TPU v7x, 32 devices: a whole 2x2x4 slice. The times are simulated.
32 devices in a mesh: groups: 2 (over y), col: 4 (over z), row: 4 (over x, core).
Axes of the slice: x: 2, y: 2, z: 4, core: 2. Of those that a mesh axis runs over, the one named last changes fastest.
Arguments:
- pair_slab: bfloat16 [128, 512, 128], P(('groups', 'row'), 'col'), parts along dimension 0, may hold values from -6 to 6
- tile_pair: bfloat16 [8, 2, 128, 128, 128], P(('groups', 'col'), None, 'row'), parts along dimension 0, may hold values from -6 to 6
- tile_cotan: bfloat16 [8, 2, 128, 128, 128], P(('groups', 'col'), None, 'row'), parts along dimension 0, may hold values from -6 to 6
- tile_rows: int32 [8, 2], P(('groups', 'col')), parts along dimension 0, may hold values from 0 to 3, as said below
- tile_count: int32 [8], P(('groups', 'col')), parts along dimension 0, may hold values from 1 to 2, as said below
- norm_gain: float32 [128], replicated, may hold values from 0.5 to 1.5
- norm_bias: float32 [128], replicated, may hold values from -2.5 to 2.5
- w_in: bfloat16 [128, 512], replicated, may hold values from -0.5 to 0.5
- out_gain: float32 [128], replicated, may hold values from 0.5 to 1.5
- out_bias: float32 [128], replicated, may hold values from -2.5 to 2.5
- w_out: bfloat16 [128, 128], replicated, may hold values from -0.5 to 0.5
- w_gate: bfloat16 [128, 128], replicated, may hold values from -0.5 to 0.5
Outputs:
- update: bfloat16 [8, 2, 128, 128, 128], P(('groups', 'col'), None, 'row'), parts along dimension 0
- grad_slab: bfloat16 [128, 512, 128], P(('groups', 'row'), 'col'), parts along dimension 0
- grad_tiles: bfloat16 [8, 2, 128, 128, 128], P(('groups', 'col'), None, 'row'), parts along dimension 0
- grad_in_w: float32 [256, 512], P('groups'), parts along dimension 0
- grad_out_w: float32 [256, 128], P('groups'), parts along dimension 0
- grad_gate_w: float32 [256, 128], P('groups'), parts along dimension 0
There are 2 independent parts, one for each index of `groups`. A program takes and returns all parts, laid end to end along the dimension named above; an argument that names none is the same for every part. Nothing has to cross between parts.
Inputs may be any that keep to these rules, and one draw needn't show every extreme that they name: `tile_count`: every column block has at least one active slot and some column block has all 2 active. `tile_rows`: the row blocks named by the slots of one column block are distinct; slots at or past the count are inactive.
All inputs are finite; a program needn't handle non-finite values.
Results may differ from a plain program's by a relative error of at most 0.015.
Values may be sent and summed in bfloat16 or wider, within the bound.
A program may use at most 128 MiB of HBM per device.

v0:
```python
import jax
import jax.numpy as jnp
from jax import lax
from jax.sharding import PartitionSpec as P

epsilon = 1e-05


def normalize(values):
    center = values - jnp.mean(values, axis=-1, keepdims=True)
    variance = jnp.mean(center * center, axis=-1, keepdims=True)
    inverse = lax.rsqrt(variance + epsilon)
    return (center * inverse, inverse)


def norm_back(grad_in, centred, inverse, gain):
    scaled = grad_in * gain
    first = jnp.mean(scaled, axis=-1, keepdims=True)
    second = jnp.mean(scaled * centred, axis=-1, keepdims=True)
    return inverse * (scaled - first - centred * second)


def rounded(values):
    return lax.optimization_barrier(values.astype(jnp.bfloat16)).astype(jnp.float32)


def body(
    pair_slab,
    tile_pair,
    tile_cotan,
    tile_rows,
    tile_count,
    norm_gain,
    norm_bias,
    w_in,
    out_gain,
    out_bias,
    w_out,
    w_gate,
):
    k_local, tile_len, channels = pair_slab.shape
    hidden_w = w_out.shape[0]
    slots = tile_rows.shape[1]
    row_count = lax.axis_size("row")
    col_count = lax.axis_size("col")
    row_part = tile_len // row_count
    slab_hat, slab_inv = normalize(pair_slab.astype(jnp.float32))
    slab_norm = (slab_hat * norm_gain + norm_bias).astype(jnp.bfloat16)
    flat_norm = slab_norm.reshape(-1, channels)
    project = jnp.dot(flat_norm, w_in, preferred_element_type=jnp.float32).reshape(
        k_local, tile_len, 4 * hidden_w
    )
    left_proj = project[..., :hidden_w]
    left_sig = jax.nn.sigmoid(project[..., hidden_w : 2 * hidden_w])
    right_proj = project[..., 2 * hidden_w : 3 * hidden_w]
    right_sig = jax.nn.sigmoid(project[..., 3 * hidden_w :])
    left_edges = (left_sig * left_proj).astype(jnp.bfloat16)
    right_edges = (right_sig * right_proj).astype(jnp.bfloat16)
    row_blocks = tile_rows[0]
    active = (jnp.arange(slots) < tile_count[0]).astype(jnp.float32)
    selector = (row_blocks[:, None] == jnp.arange(col_count)[None, :]).astype(jnp.float32) * active[
        :, None
    ]
    spread = lax.all_to_all(
        left_edges.reshape(k_local, row_count, row_part, hidden_w),
        "row",
        split_axis=1,
        concat_axis=0,
        tiled=True,
    )
    panels = lax.all_gather(spread, "col", axis=1, tiled=True)
    chosen = jnp.take(panels, row_blocks, axis=1)
    right_full = lax.all_gather(right_edges, "row", axis=0, tiled=True)
    grouped = jnp.einsum(
        "gksih,gkjh->gsijh",
        chosen.reshape(row_count, k_local, slots, row_part, hidden_w),
        right_full.reshape(row_count, k_local, tile_len, hidden_w),
        preferred_element_type=jnp.float32,
    )
    combined = jnp.sum(rounded(grouped), axis=0)
    comb_hat, comb_inv = normalize(combined)
    comb_norm = (comb_hat * out_gain + out_bias).astype(jnp.bfloat16)
    pair_hat, pair_inv = normalize(tile_pair[0].astype(jnp.float32))
    pair_norm = (pair_hat * norm_gain + norm_bias).astype(jnp.bfloat16)
    flat_comb = comb_norm.reshape(-1, hidden_w)
    flat_pair = pair_norm.reshape(-1, channels)
    mixed = jnp.dot(flat_comb, w_out, preferred_element_type=jnp.float32)
    gate = jax.nn.sigmoid(jnp.dot(flat_pair, w_gate, preferred_element_type=jnp.float32))
    row_mask = jnp.repeat(active, row_part * tile_len)[:, None]
    update = (row_mask * gate * mixed).astype(jnp.bfloat16)
    cotan = tile_cotan[0].astype(jnp.float32).reshape(-1, channels) * row_mask
    grad_mixed = (cotan * gate).astype(jnp.bfloat16)
    grad_logit = (cotan * mixed * gate * (1.0 - gate)).astype(jnp.bfloat16)
    grad_out_w = jnp.dot(flat_comb.T, grad_mixed, preferred_element_type=jnp.float32)
    grad_gate_w = jnp.dot(flat_pair.T, grad_logit, preferred_element_type=jnp.float32)
    out_total, gate_total = (grad_out_w, grad_gate_w)
    grad_comb = jnp.dot(grad_mixed, w_out.T, preferred_element_type=jnp.float32).reshape(
        slots, row_part, tile_len, hidden_w
    )
    grad_pair = jnp.dot(grad_logit, w_gate.T, preferred_element_type=jnp.float32).reshape(
        slots, row_part, tile_len, channels
    )
    pair_back = norm_back(grad_pair, pair_hat, pair_inv, norm_gain).astype(jnp.bfloat16)
    comb_back = norm_back(grad_comb, comb_hat, comb_inv, out_gain).astype(jnp.bfloat16)
    left_term = rounded(
        jnp.einsum("sijh,kjh->ksih", comb_back, right_full, preferred_element_type=jnp.float32)
    )
    routed = jnp.einsum("ksih,sb->kbih", left_term, selector)
    column_sum = lax.psum_scatter(
        routed.astype(jnp.bfloat16), "col", scatter_dimension=1, tiled=True
    ).astype(jnp.float32)
    returned = lax.all_to_all(
        column_sum.reshape(row_count, k_local, row_part, hidden_w).astype(jnp.bfloat16),
        "row",
        split_axis=0,
        concat_axis=2,
        tiled=True,
    ).astype(jnp.float32)
    left_grad = returned.reshape(k_local, tile_len, hidden_w)
    right_part = jnp.einsum(
        "sijh,ksih->skjh", comb_back, chosen, preferred_element_type=jnp.float32
    )
    right_grad = jnp.sum(
        lax.psum_scatter(
            right_part.astype(jnp.bfloat16), "row", scatter_dimension=1, tiled=True
        ).astype(jnp.float32),
        axis=0,
    )
    grad_project = jnp.concatenate(
        [
            left_grad * left_sig,
            left_grad * left_proj * left_sig * (1.0 - left_sig),
            right_grad * right_sig,
            right_grad * right_proj * right_sig * (1.0 - right_sig),
        ],
        axis=-1,
    ).astype(jnp.bfloat16)
    flat_grad = grad_project.reshape(-1, 4 * hidden_w)
    grad_in_w = jnp.dot(flat_norm.T, flat_grad, preferred_element_type=jnp.float32)
    grad_norm = jnp.dot(flat_grad, w_in.T, preferred_element_type=jnp.float32).reshape(
        k_local, tile_len, channels
    )
    grad_slab = norm_back(grad_norm, slab_hat, slab_inv, norm_gain).astype(jnp.bfloat16)
    in_total, out_total, gate_total = lax.psum((grad_in_w, out_total, gate_total), ("col", "row"))
    update_out = update.reshape(1, slots, row_part, tile_len, channels)
    tiles_out = pair_back.reshape(1, slots, row_part, tile_len, channels)
    return (update_out, grad_slab, tiles_out, in_total, out_total, gate_total)


def solution(mesh):
    return jax.shard_map(
        body,
        mesh=mesh,
        in_specs=(
            P(("groups", "row"), "col", None),
            P(("groups", "col"), None, "row", None, None),
            P(("groups", "col"), None, "row", None, None),
            P(("groups", "col"), None),
            P(("groups", "col")),
            P(),
            P(),
            P(),
            P(),
            P(),
            P(),
            P(),
        ),
        out_specs=(
            P(("groups", "col"), None, "row", None, None),
            P(("groups", "row"), "col", None),
            P(("groups", "col"), None, "row", None, None),
            P("groups", None),
            P("groups", None),
            P("groups", None),
        ),
        check_vma=False,
    )
```

profile of v0, /device:TPU:0, one launch (start us, length us, event | category | flops | bytes accessed | tf_op | source)
XLA Modules:
  0.0 365.0 jit_solution(873537648331085904)
XLA Ops:
  7.2 1.3 copy.55
  8.7 0.2 fusion.25
  8.9 1.5 fusion.33
  10.4 1.9 copy-done.1
  12.3 1.3 multiply_convert_fusion.7
  13.7 0.8 copy.57
  14.5 4.2 %all-to-all-start = ((bf16[16,4,32,128]{3,2,0,1:T(8,128)(2,1)}), bf16[16,4,32,128]{3,2,0,1:T(8,128)(2,1)S(1)}, u32[]{:S(2)}, u32[]{:S(2)}) async-start(bf16[16,4,32,128]{3,2,0,1:T(8,128)(2,1)} %copy.57), calls=%async_computation | async-start | bytes 1048576 | tf_op jit(solution)/shard_map/all_to_all | solution.py:64
  19.5 9.8 %all-to-all-done = bf16[16,4,32,128]{3,2,0,1:T(8,128)(2,1)S(1)} async-done(((bf16[16,4,32,128]{3,2,0,1:T(8,128)(2,1)}), bf16[16,4,32,128]{3,2,0,1:T(8,128)(2,1)S(1)}, u32[]{:S(2)}, u32[]{:S(2)}) %all-to-all-start) | async-done | bytes 524320 | tf_op jit(solution)/shard_map/all_to_all | solution.py:64
  29.3 0.8 copy-done.11
  30.2 0.6 convert_reduce_fusion.2
  30.9 2.5 fusion.11
  33.4 3.5 add_convert_fusion.1
  36.9 3.4 all-gather.3.cloned.1.call-done
  40.3 4.5 %copy.74 = bf16[4,16,128,128,1]{2,1,4,3,0:T(8,128)(2,1)} copy(bf16[4,16,128,128,1]{3,2,1,0,4:T(8,128)(2,1)} %bitcast.112) | data formatting | bytes 4194304 | tf_op jit(solution)/shard_map/reshape | solution.py:77
  44.8 4.2 %copy.75 = bf16[64,128,128,1]{1,0,3,2:T(8,128)(2,1)} copy(bf16[64,128,128,1]{2,1,0,3:T(8,128)(2,1)} %bitcast.113) | data formatting | bytes 4194304 | tf_op jit(solution)/shard_map/all_gather | solution.py:73
  49.0 40.4 %all-gather.5.cloned.1.call-done = bf16[64,4,32,128]{3,2,1,0:T(8,128)(2,1)} async-done(((bf16[64,1,32,128]{3,2,1,0:T(8,128)(2,1)}), bf16[64,4,32,128]{3,2,1,0:T(8,128)(2,1)}) %all-gather.5.cloned.1.call-update) | async-done | bytes 2097168 | tf_op jit(solution)/shard_map/all_gather | solution.py:71
  89.5 3.3 gather_fusion
  92.7 1.4 copy.59
  94.1 1.1 broadcast_select_fusion.1
  95.2 7.2 %copy.61 = bf16[4,16,2,32,128]{3,1,2,4,0:T(8,128)(2,1)} copy(bf16[4,16,2,32,128]{4,3,2,1,0:T(8,128)(2,1)} %broadcast_select_fusion.1) | data formatting | bytes 2097152 | tf_op jit(solution)/shard_map/jit(_take)/select_n | solution.py:72
  102.4 5.2 %convert_bitcast_fusion = bf16[4,2,32,128,128]{3,2,1,4,0:T(8,128)(2,1)S(1)} fusion(bf16[4,16,128,128,1]{2,1,4,3,0:T(8,128)(2,1)} %copy.74, bf16[4,16,2,32,128]{3,1,2,4,0:T(8,128)(2,1)} %copy.61), kind=kOutput, calls=%fused_computation.7 | convolution fusion | flops 138412032 | bytes 11534336 | tf_op jit(solution)/shard_map/gksih,gkjh->gsijh/dot_general | solution.py:74
  107.7 5.1 %convert_reduce_fusion = (f32[2,32,128]{2,1,0:T(8,128)S(1)}, f32[2,32,128,128]{2,1,0,3:T(8,128)}) fusion(bf16[4,2,32,128,128]{3,2,1,4,0:T(8,128)(2,1)S(1)} %convert_bitcast_fusion), kind=kLoop, calls=%fused_computation.1 | loop fusion | flops 11526144 | bytes 12615680 | tf_op jit(solution)/shard_map/reduce_sum | solution.py:10
  112.7 5.3 %copy.62 = f32[2,32,128,128]{3,2,1,0:T(8,128)} copy(f32[2,32,128,128]{2,1,0,3:T(8,128)} %get-tuple-element.31) | data formatting | bytes 8388608 | tf_op jit(solution)/shard_map/reduce_sum | solution.py:80
  118.1 2.8 multiply_reduce_fusion.2
  120.9 0.6 copy-done.2
  121.5 4.5 %add_convert_fusion = bf16[8192,128]{1,0:T(8,128)(2,1)S(1)} fusion(f32[2,32,128,128]{3,2,1,0:T(8,128)S(1)} %copy-done.2, f32[128]{0:T(128)S(1)} %copy-done.18, f32[128]{0:T(128)S(1)} %copy-done.15, f32[8192]{0:T(1024)S(1)} %bitcast.123, f32[8192]{0:T(1024)S(1)} %bitcast.119), kind=kLoop, calls=%fused_computation.28 | loop fusion | flops 5242880 | bytes 6358016 | tf_op jit(solution)/shard_map/convert_element_type | solution.py:82
  126.1 0.7 fusion.48
  126.8 0.6 copy-done.4
  127.4 1.0 copy-done.7
  128.4 0.6 copy-done.19
  129.1 4.3 %fusion.8 = (bf16[8192,128]{1,0:T(8,128)(2,1)}, bf16[8192,128]{1,0:T(8,128)(2,1)}, bf16[8192,128]{1,0:T(8,128)(2,1)S(1)}) fusion(f32[8192,128]{1,0:T(8,128)S(1)} %fusion.48, bf16[1,2,32,128,128]{4,3,2,1,0:T(8,128)(2,1)S(1)} %copy-done.19, f32[8192]{0:T(1024)S(1)} %bitcast.132, bf16[8192,128]{1,0:T(8,128)(2,1)S(1)} %copy-done.7, ...), kind=kOutput, calls=%fused_computation.14 | convolution fusion | flops 284164096 | bytes 14745600 | tf_op jit(solution)/shard_map/dot_general | solution.py:88
  133.4 6.2 %multiply_reduce_fusion.4 = (f32[8192]{0:T(1024)S(1)}, f32[8192]{0:T(1024)S(1)}, f32[8192,128]{1,0:T(8,128)}) fusion(f32[128]{0:T(128)S(1)} %copy-done.15, f32[8192]{0:T(1024)S(1)} %bitcast.124, f32[8192]{0:T(1024)S(1)} %bitcast.120, f32[2,32,128,128]{3,2,1,0:T(8,128)S(1)} %copy-done.2, bf16[8192,128]{1,0:T(8,128)(2,1)S(1)} %get-tuple-element.43, ...), kind=kOutput, calls=%fused_computation.32 | convolution fusion | flops 274710528 | bytes 10650112 | tf_op jit(solution)/shard_map/dot_general | solution.py:97
  139.6 5.5 %copy.63 = f32[2,32,128,128]{2,1,0,3:T(8,128)} copy(f32[2,32,128,128]{3,2,1,0:T(8,128)} %bitcast.110) | data formatting | bytes 8388608 | tf_op jit(solution)/shard_map/reshape | solution.py:97
  145.1 4.8 %multiply_convert_fusion.1 = bf16[2,32,128,128]{2,1,0,3:T(8,128)(2,1)S(1)} fusion(f32[2,32,128,128]{2,1,0,3:T(8,128)} %copy.63, f32[2,32,128,128]{2,1,0,3:T(8,128)} %get-tuple-element.31, f32[2,32,128]{2,1,0:T(8,128)S(1)} %bitcast.128, f32[2,32,128]{2,1,0:T(8,128)S(1)} %bitcast.129, f32[128]{0:T(128)S(1)} %copy-done.15, f32[2,32,128]{2,1,0:T(8,128)S(1)} %add_rsqrt_fusion, ...), kind=kLoop, calls=%fused_computation.25 | loop fusion | flops 8388608 | bytes 10617344 | tf_op jit(solution)/shard_map/convert_element_type | solution.py:104
  149.9 1.4 copy-done.5
  151.3 2.5 convert_bitcast_fusion.3
  153.8 4.7 %copy.65 = bf16[64,2,32,128]{3,1,2,0:T(2,128)(2,1)} copy(bf16[64,2,32,128]{0,2,1,3:T(8,128)(2,1)} %convert_bitcast_fusion.3) | data formatting | bytes 2097152 | tf_op jit(solution)/shard_map/optimization_barrier | solution.py:24
  158.5 2.8 convert_bitcast_fusion.2
  161.3 1.7 copy.66
  163.1 2.4 broadcast_select_fusion
  165.4 5.4 %copy.68 = bf16[64,2,32,128]{0,2,3,1:T(8,128)(2,1)} copy(bf16[64,2,32,128]{3,2,0,1:T(8,128)(2,1)} %broadcast_select_fusion) | data formatting | bytes 2097152 | tf_op jit(solution)/shard_map/jit(_take)/select_n | solution.py:72
  170.8 5.5 %convert_bitcast_fusion.1 = bf16[2,64,128,128]{2,1,3,0:T(8,128)(2,1)} fusion(bf16[64,2,32,128]{0,2,3,1:T(8,128)(2,1)} %copy.68, bf16[2,32,128,128]{2,1,0,3:T(8,128)(2,1)} %copy-done.5), kind=kOutput, calls=%fused_computation.24 | convolution fusion | flops 136314880 | bytes 7340032 | tf_op jit(solution)/shard_map/sijh,ksih->skjh/dot_general | solution.py:120
  176.3 7.2 %multiply_reduce_fusion.3 = (f32[8192]{0:T(1024)S(1)}, f32[8192]{0:T(1024)S(1)}, f32[8192,128]{1,0:T(8,128)S(1)}) fusion(f32[128]{0:T(128)S(1)} %copy-done.16, f32[8192]{0:T(1024)S(1)} %bitcast.127, f32[8192]{0:T(1024)S(1)} %bitcast.122, bf16[1,2,32,128,128]{4,3,2,1,0:T(8,128)(2,1)S(1)} %copy-done.3, bf16[8192,128]{1,0:T(8,128)(2,1)} %get-tuple-element.41, ...), kind=kOutput, calls=%fused_computation.31 | convolution fusion | flops 275759104 | bytes 8552960 | tf_op jit(solution)/shard_map/dot_general | solution.py:100
  183.5 5.9 %multiply_convert_fusion = bf16[1,2,32,128,128]{4,3,2,1,0:T(8,128)(2,1)} fusion(f32[1,2,32,128,128]{4,3,2,1,0:T(8,128)S(1)} %bitcast.115, bf16[1,2,32,128,128]{4,3,2,1,0:T(8,128)(2,1)S(1)} %copy-done.3, f32[2,32,128]{2,1,0:T(8,128)S(1)} %bitcast.130, f32[2,32,128]{2,1,0:T(8,128)S(1)} %broadcast_multiply_fusion.5, f32[2,32,128]{2,1,0:T(8,128)S(1)} %bitcast.131, ...), kind=kLoop, calls=%fused_computation.22 | loop fusion | flops 9437184 | bytes 8520192 | tf_op jit(solution)/shard_map/convert_element_type | solution.py:103
  189.5 16.3 %reduce-scatter.3.cloned.1.call-done = bf16[64,1,32,128]{3,2,0,1:T(8,128)(2,1)} async-done(((bf16[64,4,32,128]{3,2,0,1:T(8,128)(2,1)}), bf16[64,1,32,128]{3,2,0,1:T(8,128)(2,1)}) %reduce-scatter.3.cloned.1.call-update) | async-done | bytes 524304 | tf_op jit(solution)/shard_map/reduce_scatter | solution.py:109
  205.8 3.5 all-to-all-start.1
  209.2 0.3 all-reduce.3.cloned.1.call-start
  209.6 3.8 %fusion.49 = f32[128,128]{1,0:T(8,128)} fusion(bf16[8192,128]{1,0:T(8,128)(2,1)} %copy-done.4, bf16[8192,128]{1,0:T(8,128)(2,1)} %copy-done.9), kind=kOutput, calls=%fused_computation.105 | convolution fusion | flops 268435456 | bytes 4259840 | tf_op jit(solution)/shard_map/dot_general | solution.py:94
  213.3 1.4 fusion.50
  214.7 3.4 all-to-all-done.1
  218.0 0.1 convert_bitcast_fusion.4
  218.3 33.9 %reduce-scatter.5.cloned.1.call-done = bf16[2,16,128,128]{2,1,3,0:T(8,128)(2,1)} async-done(((bf16[2,64,128,128]{2,1,3,0:T(8,128)(2,1)}), bf16[2,16,128,128]{2,1,3,0:T(8,128)(2,1)}) %reduce-scatter.5.cloned.1.call-update) | async-done | bytes 1048592 | tf_op jit(solution)/shard_map/reduce_scatter | solution.py:124
  252.2 1.5 convert_reduce_fusion.3
  253.7 1.4 copy.70
  255.0 3.6 multiply_convert_fusion.6
  258.7 0.8 copy-done.13
  259.4 1.2 convolution_bitcast_fusion
  260.6 2.0 fusion.47
  262.7 0.3 fusion.24
  263.0 1.0 copy.72
  264.0 89.8 %all-reduce.3.cloned.1.call-done = (f32[128,512]{1,0:T(8,128)}, f32[128,128]{1,0:T(8,128)}, f32[128,128]{1,0:T(8,128)}) async-done(((f32[128,512]{1,0:T(8,128)}, f32[128,128]{1,0:T(8,128)}, f32[128,128]{1,0:T(8,128)}), (f32[128,512]{1,0:T(8,128)}, f32[128,128]{1,0:T(8,128)}, f32[128,128]{1,0:T(8,128)})) %all-reduce.3.cloned.1.call-update) | async-done | bytes 393232 | tf_op jit(solution)/shard_map/psum | solution.py:144
  353.8 1.7 copy.88
  355.5 1.5 copy.89
  357.0 1.5 copy.90
  (63 shorter events, 0.6 us)
Async XLA Ops:
  7.2 1.7 copy-start
  7.2 33.2 %all-gather.3.cloned.1.call-start = ((), (), s32[]{:S(2)}) async-start(), calls=%async_computation.4 | async-start | bytes 2621440 | tf_op jit(solution)/shard_map/all_gather | solution.py:73
  10.4 1.9 copy-start.1
  12.3 7.2 %copy-start.21 = (s32[1,2]{1,0:T(1,128)S(1)}, s32[1,2]{1,0:T(1,128)}, u32[]{:S(2)}) copy-start(s32[1,2]{1,0:T(1,128)} %param.15) | copy-start | bytes 28
  12.3 17.9 %copy-start.3 = (bf16[1,2,32,128,128]{4,3,2,1,0:T(8,128)(2,1)S(1)}, bf16[1,2,32,128,128]{4,3,2,1,0:T(8,128)(2,1)}, u32[]{:S(2)}) copy-start(bf16[1,2,32,128,128]{4,3,2,1,0:T(8,128)(2,1)} %param.13) | copy-start | bytes 6291460
  13.7 19.8 %copy-start.16 = (f32[128]{0:T(128)S(1)}, f32[128]{0:T(128)}, u32[]{:S(2)}) copy-start(f32[128]{0:T(128)} %param.17) | copy-start | bytes 1540
  13.7 19.8 %copy-start.17 = (f32[128]{0:T(128)S(1)}, f32[128]{0:T(128)}, u32[]{:S(2)}) copy-start(f32[128]{0:T(128)} %param.18) | copy-start | bytes 1540
  14.5 14.8 %all-to-all-start = ((bf16[16,4,32,128]{3,2,0,1:T(8,128)(2,1)}), bf16[16,4,32,128]{3,2,0,1:T(8,128)(2,1)S(1)}, u32[]{:S(2)}, u32[]{:S(2)}) async-start(bf16[16,4,32,128]{3,2,0,1:T(8,128)(2,1)} %copy.57), calls=%async_computation | async-start | bytes 1048576 | tf_op jit(solution)/shard_map/all_to_all | solution.py:64
  18.7 70.7 %all-gather.5.cloned.1.call-start = ((), (), s32[]{:S(2)}) async-start(), calls=%async_computation.5 | async-start | bytes 2621440 | tf_op jit(solution)/shard_map/all_gather | solution.py:71
  29.3 0.8 copy-start.11
  30.1 175.6 %reduce-scatter.3.cloned.1.call-start = ((), (), s32[]{:S(2)}) async-start(), calls=%async_computation.6 | async-start | bytes 2621440 | tf_op jit(solution)/shard_map/reduce_scatter | solution.py:109
  118.1 3.4 copy-start.2
  118.1 3.4 copy-start.15
  118.1 3.5 copy-start.18
  120.9 5.2 %copy-start.14 = (bf16[128,128]{1,0:T(8,128)(2,1)S(1)}, bf16[128,128]{1,0:T(8,128)(2,1)}, u32[]{:S(2)}) copy-start(bf16[128,128]{1,0:T(8,128)(2,1)} %param.22) | copy-start | bytes 98308
  126.1 1.3 copy-start.4
  126.1 2.3 copy-start.7
  126.1 3.0 copy-start.19
  126.1 3.0 copy-start.20
  133.4 6.2 %copy-start.9 = (bf16[8192,128]{1,0:T(8,128)(2,1)}, bf16[8192,128]{1,0:T(8,128)(2,1)S(1)}, u32[]{:S(2)}) copy-start(bf16[8192,128]{1,0:T(8,128)(2,1)S(1)} %get-tuple-element.43) | copy-start | bytes 6291460
  145.1 6.2 %copy-start.6 = (bf16[64,128,128,1]{1,0,3,2:T(8,128)(2,1)S(1)}, bf16[64,128,128,1]{1,0,3,2:T(8,128)(2,1)}, u32[]{:S(2)}) copy-start(bf16[64,128,128,1]{1,0,3,2:T(8,128)(2,1)} %copy.75) | copy-start | bytes 6291460
  149.9 1.4 copy-start.5
  163.0 89.1 %reduce-scatter.5.cloned.1.call-start = ((), (), s32[]{:S(2)}) async-start(), calls=%async_computation.7 | async-start | bytes 5242880 | tf_op jit(solution)/shard_map/reduce_scatter | solution.py:124
  189.5 23.9 %copy-start.8 = (bf16[8192,128]{1,0:T(8,128)(2,1)S(1)}, bf16[8192,128]{1,0:T(8,128)(2,1)}, u32[]{:S(2)}) copy-start(bf16[8192,128]{1,0:T(8,128)(2,1)} %add_convert_fusion.1) | copy-start | bytes 6291460
  205.8 12.3 %all-to-all-start.1 = ((bf16[4,16,32,128]{3,2,1,0:T(8,128)(2,1)}), bf16[4,16,32,128]{3,2,1,0:T(8,128)(2,1)S(1)}, u32[]{:S(2)}, u32[]{:S(2)}) async-start(bf16[4,16,32,128]{3,2,1,0:T(8,128)(2,1)} %bitcast.125), calls=%async_computation.2 | async-start | bytes 1048576 | tf_op jit(solution)/shard_map/all_to_all | solution.py:112
  209.2 144.6 %all-reduce.3.cloned.1.call-start = ((), (), s32[]{:S(2)}) async-start(), calls=%async_computation.8 | async-start | bytes 786432 | tf_op jit(solution)/shard_map/psum | solution.py:144
  209.5 3.8 %copy-start.10 = (bf16[8192,128]{1,0:T(8,128)(2,1)S(1)}, bf16[8192,128]{1,0:T(8,128)(2,1)}, u32[]{:S(2)}) copy-start(bf16[8192,128]{1,0:T(8,128)(2,1)} %get-tuple-element.41) | copy-start | bytes 6291460
  258.6 0.8 copy-start.13
  258.7 2.0 copy-start.12
Sparse Core Ops, SparseCore 0:
  13.8 26.4 all-gather.2
  42.5 46.9 all-gather.4
  163.1 42.5 reduce-scatter.2
  208.3 43.8 reduce-scatter.4
  262.8 90.9 all-reduce.2
where the time goes:
time: 366 us; the launch traced here: 365 us
  waiting for transfers between devices  197 us (54%)
  local copies, waits for them, and re-layouts  60.2 us (16%)
  matrix products  44.3 us (12%)
  other arithmetic  40.4 us (11%)
  between operations  14.8 us (4%)
  starting transfers between devices  8.1 us (2%)
    psum x1, waiting for transfers between devices, body(): lax.psum((grad_in_w, out_total, gate_total), ('col', 'row'))  89.8 us
    all_gather x1, waiting for transfers between devices, body(): panels = lax.all_gather(spread, 'col', axis=1, tiled=True)  40.4 us
    reduce_scatter x1, waiting for transfers between devices, body(): lax.psum_scatter(right_part.astype(jnp.bfloat16), 'row', scatter_dimensio...  33.9 us
    reduce_scatter x1, waiting for transfers between devices, body(): lax.psum_scatter(routed.astype(jnp.bfloat16), 'col', scatter_dimension=1,...  16.3 us
    unnamed x51, local copies, waits for them, and re-layouts  14.8 us
    select_n x2, local copies, waits for them, and re-layouts, body(): chosen = jnp.take(panels, row_blocks, axis=1)  12.6 us
    all_to_all x1, waiting for transfers between devices, body(): lax.all_to_all(left_edges.reshape(k_local, row_count, row_part, hidden_w)...  9.82 us
  transfers between devices with their start and end apart: 7, of which 7 were waited for; matrix products, arithmetic and copies ran while one was open for 14% of the time, Pallas kernels for 0%

commit v1 on v0

--- a/solution.py
+++ b/solution.py
@@ -61,12 +61,20 @@
     selector = (row_blocks[:, None] == jnp.arange(col_count)[None, :]).astype(jnp.float32) * active[
         :, None
     ]
-    spread = lax.all_to_all(
-        left_edges.reshape(k_local, row_count, row_part, hidden_w),
-        "row",
-        split_axis=1,
-        concat_axis=0,
-        tiled=True,
+    spread = jnp.concatenate(
+        lax.all_to_all(
+            jnp.stack(
+                jnp.split(
+                    left_edges.reshape(k_local, row_count, row_part, hidden_w),
+                    lax.axis_size("row"),
+                    axis=1,
+                )
+            ),
+            "row",
+            0,
+            0,
+        ),
+        axis=0,
     )
     panels = lax.all_gather(spread, "col", axis=1, tiled=True)
     chosen = jnp.take(panels, row_blocks, axis=1)

time: 366 us -> 366 us (level)
  no operation moved by 1% of the time
where the time goes in v1:
time: 366 us; the launch traced here: 365 us
  waiting for transfers between devices  197 us (54%)
  local copies, waits for them, and re-layouts  59.4 us (16%)
  matrix products  44.3 us (12%)
  other arithmetic  41.3 us (11%)
  between operations  14.8 us (4%)
  starting transfers between devices  8.1 us (2%)
    psum x1, waiting for transfers between devices, body(): lax.psum((grad_in_w, out_total, gate_total), ('col', 'row'))  89.8 us
    all_gather x1, waiting for transfers between devices, body(): panels = lax.all_gather(spread, 'col', axis=1, tiled=True)  40.4 us
    reduce_scatter x1, waiting for transfers between devices, body(): lax.psum_scatter(right_part.astype(jnp.bfloat16), 'row', scatter_dimensio...  33.9 us
    reduce_scatter x1, waiting for transfers between devices, body(): lax.psum_scatter(routed.astype(jnp.bfloat16), 'col', scatter_dimension=1,...  16.3 us
    unnamed x51, local copies, waits for them, and re-layouts  14.8 us
    select_n x2, local copies, waits for them, and re-layouts, body(): chosen = jnp.take(panels, row_blocks, axis=1)  12.6 us
    all_to_all x1, waiting for transfers between devices, body(): lax.all_to_all(jnp.stack(jnp.split(left_edges.reshape(k_local, row_count,...  9.92 us
  transfers between devices with their start and end apart: 7, of which 7 were waited for; matrix products, arithmetic and copies ran while one was open for 14% of the time, Pallas kernels for 0%

profile of v1, /device:TPU:0, one launch (start us, length us, event | category | flops | bytes accessed | tf_op | source)
XLA Modules:
  0.0 365.0 jit_solution(13779066549046208919)
XLA Ops:
  7.2 1.3 copy.60
  8.7 0.2 fusion.25
  8.9 1.5 fusion.33
  10.4 1.9 copy-done.1
  12.3 1.3 multiply_convert_fusion.7
  13.7 0.9 pad_maximum_fusion.1
  14.6 4.2 %all-to-all-start = ((bf16[4,16,1,32,128]{4,3,1,2,0:T(8,128)(2,1)}), bf16[4,16,1,32,128]{4,3,1,2,0:T(8,128)(2,1)S(1)}, u32[]{:S(2)}, u32[]{:S(2)}) async-start(bf16[4,16,1,32,128]{4,3,1,2,0:T(8,128)(2,1)} %pad_maximum_fusion.1), calls=%async_computation | async-start | bytes 1048576 | tf_op jit(solution)/shard_map/all_to_all | solution.py:65
  19.6 9.9 %all-to-all-done = bf16[4,16,1,32,128]{4,3,1,2,0:T(8,128)(2,1)S(1)} async-done(((bf16[4,16,1,32,128]{4,3,1,2,0:T(8,128)(2,1)}), bf16[4,16,1,32,128]{4,3,1,2,0:T(8,128)(2,1)S(1)}, u32[]{:S(2)}, u32[]{:S(2)}) %all-to-all-start) | async-done | bytes 524320 | tf_op jit(solution)/shard_map/all_to_all | solution.py:65
  29.5 0.8 copy-done.11
  30.4 0.6 convert_reduce_fusion.2
  31.0 2.5 fusion.11
  33.6 3.5 add_convert_fusion.1
  37.1 3.3 all-gather.3.cloned.1.call-done
  40.4 4.5 %copy.80 = bf16[4,16,128,128,1]{2,1,4,3,0:T(8,128)(2,1)} copy(bf16[4,16,128,128,1]{3,2,1,0,4:T(8,128)(2,1)} %bitcast.120) | data formatting | bytes 4194304 | tf_op jit(solution)/shard_map/reshape | solution.py:85
  44.9 4.2 %copy.81 = bf16[64,128,128,1]{1,0,3,2:T(8,128)(2,1)} copy(bf16[64,128,128,1]{2,1,0,3:T(8,128)(2,1)} %bitcast.121) | data formatting | bytes 4194304 | tf_op jit(solution)/shard_map/all_gather | solution.py:81
  49.1 40.4 %all-gather.5.cloned.1.call-done = bf16[64,4,32,128]{3,2,1,0:T(8,128)(2,1)} async-done(((bf16[64,1,32,128]{3,2,1,0:T(8,128)(2,1)}), bf16[64,4,32,128]{3,2,1,0:T(8,128)(2,1)}) %all-gather.5.cloned.1.call-update) | async-done | bytes 2097168 | tf_op jit(solution)/shard_map/all_gather | solution.py:79
  89.5 3.3 gather_fusion
  92.8 1.4 copy.65
  94.2 1.1 broadcast_select_fusion.1
  95.3 7.2 %copy.67 = bf16[4,16,2,32,128]{3,1,2,4,0:T(8,128)(2,1)} copy(bf16[4,16,2,32,128]{4,3,2,1,0:T(8,128)(2,1)} %broadcast_select_fusion.1) | data formatting | bytes 2097152 | tf_op jit(solution)/shard_map/jit(_take)/select_n | solution.py:80
  102.5 5.2 %convert_bitcast_fusion = bf16[4,2,32,128,128]{3,2,1,4,0:T(8,128)(2,1)S(1)} fusion(bf16[4,16,128,128,1]{2,1,4,3,0:T(8,128)(2,1)} %copy.80, bf16[4,16,2,32,128]{3,1,2,4,0:T(8,128)(2,1)} %copy.67), kind=kOutput, calls=%fused_computation.7 | convolution fusion | flops 138412032 | bytes 11534336 | tf_op jit(solution)/shard_map/gksih,gkjh->gsijh/dot_general | solution.py:82
  107.7 5.1 %convert_reduce_fusion = (f32[2,32,128]{2,1,0:T(8,128)S(1)}, f32[2,32,128,128]{2,1,0,3:T(8,128)}) fusion(bf16[4,2,32,128,128]{3,2,1,4,0:T(8,128)(2,1)S(1)} %convert_bitcast_fusion), kind=kLoop, calls=%fused_computation.1 | loop fusion | flops 11526144 | bytes 12615680 | tf_op jit(solution)/shard_map/reduce_sum | solution.py:10
  112.8 5.3 %copy.68 = f32[2,32,128,128]{3,2,1,0:T(8,128)} copy(f32[2,32,128,128]{2,1,0,3:T(8,128)} %get-tuple-element.31) | data formatting | bytes 8388608 | tf_op jit(solution)/shard_map/reduce_sum | solution.py:88
  118.2 2.8 multiply_reduce_fusion.2
  121.0 0.6 copy-done.2
  121.6 4.5 %add_convert_fusion = bf16[8192,128]{1,0:T(8,128)(2,1)S(1)} fusion(f32[2,32,128,128]{3,2,1,0:T(8,128)S(1)} %copy-done.2, f32[128]{0:T(128)S(1)} %copy-done.18, f32[128]{0:T(128)S(1)} %copy-done.15, f32[8192]{0:T(1024)S(1)} %bitcast.131, f32[8192]{0:T(1024)S(1)} %bitcast.127), kind=kLoop, calls=%fused_computation.28 | loop fusion | flops 5242880 | bytes 6358016 | tf_op jit(solution)/shard_map/convert_element_type | solution.py:90
  126.2 0.7 fusion.48
  126.9 0.6 copy-done.4
  127.5 1.0 copy-done.7
  128.5 0.6 copy-done.19
  129.2 4.3 %fusion.8 = (bf16[8192,128]{1,0:T(8,128)(2,1)}, bf16[8192,128]{1,0:T(8,128)(2,1)}, bf16[8192,128]{1,0:T(8,128)(2,1)S(1)}) fusion(f32[8192,128]{1,0:T(8,128)S(1)} %fusion.48, bf16[1,2,32,128,128]{4,3,2,1,0:T(8,128)(2,1)S(1)} %copy-done.19, f32[8192]{0:T(1024)S(1)} %bitcast.140, bf16[8192,128]{1,0:T(8,128)(2,1)S(1)} %copy-done.7, ...), kind=kOutput, calls=%fused_computation.14 | convolution fusion | flops 284164096 | bytes 14745600 | tf_op jit(solution)/shard_map/dot_general | solution.py:96
  133.5 6.2 %multiply_reduce_fusion.4 = (f32[8192]{0:T(1024)S(1)}, f32[8192]{0:T(1024)S(1)}, f32[8192,128]{1,0:T(8,128)}) fusion(f32[128]{0:T(128)S(1)} %copy-done.15, f32[8192]{0:T(1024)S(1)} %bitcast.132, f32[8192]{0:T(1024)S(1)} %bitcast.128, f32[2,32,128,128]{3,2,1,0:T(8,128)S(1)} %copy-done.2, bf16[8192,128]{1,0:T(8,128)(2,1)S(1)} %get-tuple-element.43, ...), kind=kOutput, calls=%fused_computation.32 | convolution fusion | flops 274710528 | bytes 10650112 | tf_op jit(solution)/shard_map/dot_general | solution.py:105
  139.7 5.5 %copy.69 = f32[2,32,128,128]{2,1,0,3:T(8,128)} copy(f32[2,32,128,128]{3,2,1,0:T(8,128)} %bitcast.118) | data formatting | bytes 8388608 | tf_op jit(solution)/shard_map/reshape | solution.py:105
  145.2 4.8 %multiply_convert_fusion.1 = bf16[2,32,128,128]{2,1,0,3:T(8,128)(2,1)S(1)} fusion(f32[2,32,128,128]{2,1,0,3:T(8,128)} %copy.69, f32[2,32,128,128]{2,1,0,3:T(8,128)} %get-tuple-element.31, f32[2,32,128]{2,1,0:T(8,128)S(1)} %bitcast.136, f32[2,32,128]{2,1,0:T(8,128)S(1)} %bitcast.137, f32[128]{0:T(128)S(1)} %copy-done.15, f32[2,32,128]{2,1,0:T(8,128)S(1)} %add_rsqrt_fusion, ...), kind=kLoop, calls=%fused_computation.25 | loop fusion | flops 8388608 | bytes 10617344 | tf_op jit(solution)/shard_map/convert_element_type | solution.py:112
  150.0 1.4 copy-done.5
  151.3 2.5 convert_bitcast_fusion.3
  153.9 4.7 %copy.71 = bf16[64,2,32,128]{3,1,2,0:T(2,128)(2,1)} copy(bf16[64,2,32,128]{0,2,1,3:T(8,128)(2,1)} %convert_bitcast_fusion.3) | data formatting | bytes 2097152 | tf_op jit(solution)/shard_map/optimization_barrier | solution.py:24
  158.6 2.8 convert_bitcast_fusion.2
  161.4 1.7 copy.72
  163.1 2.4 broadcast_select_fusion
  165.5 5.4 %copy.74 = bf16[64,2,32,128]{0,2,3,1:T(8,128)(2,1)} copy(bf16[64,2,32,128]{3,2,0,1:T(8,128)(2,1)} %broadcast_select_fusion) | data formatting | bytes 2097152 | tf_op jit(solution)/shard_map/jit(_take)/select_n | solution.py:80
  170.9 5.5 %convert_bitcast_fusion.1 = bf16[2,64,128,128]{2,1,3,0:T(8,128)(2,1)} fusion(bf16[64,2,32,128]{0,2,3,1:T(8,128)(2,1)} %copy.74, bf16[2,32,128,128]{2,1,0,3:T(8,128)(2,1)} %copy-done.5), kind=kOutput, calls=%fused_computation.24 | convolution fusion | flops 136314880 | bytes 7340032 | tf_op jit(solution)/shard_map/sijh,ksih->skjh/dot_general | solution.py:128
  176.4 7.2 %multiply_reduce_fusion.3 = (f32[8192]{0:T(1024)S(1)}, f32[8192]{0:T(1024)S(1)}, f32[8192,128]{1,0:T(8,128)S(1)}) fusion(f32[128]{0:T(128)S(1)} %copy-done.16, f32[8192]{0:T(1024)S(1)} %bitcast.135, f32[8192]{0:T(1024)S(1)} %bitcast.130, bf16[1,2,32,128,128]{4,3,2,1,0:T(8,128)(2,1)S(1)} %copy-done.3, bf16[8192,128]{1,0:T(8,128)(2,1)} %get-tuple-element.41, ...), kind=kOutput, calls=%fused_computation.31 | convolution fusion | flops 275759104 | bytes 8552960 | tf_op jit(solution)/shard_map/dot_general | solution.py:108
  183.6 5.9 %multiply_convert_fusion = bf16[1,2,32,128,128]{4,3,2,1,0:T(8,128)(2,1)} fusion(f32[1,2,32,128,128]{4,3,2,1,0:T(8,128)S(1)} %bitcast.123, bf16[1,2,32,128,128]{4,3,2,1,0:T(8,128)(2,1)S(1)} %copy-done.3, f32[2,32,128]{2,1,0:T(8,128)S(1)} %bitcast.138, f32[2,32,128]{2,1,0:T(8,128)S(1)} %broadcast_multiply_fusion.5, f32[2,32,128]{2,1,0:T(8,128)S(1)} %bitcast.139, ...), kind=kLoop, calls=%fused_computation.22 | loop fusion | flops 9437184 | bytes 8520192 | tf_op jit(solution)/shard_map/convert_element_type | solution.py:111
  189.5 16.3 %reduce-scatter.3.cloned.1.call-done = bf16[64,1,32,128]{3,2,0,1:T(8,128)(2,1)} async-done(((bf16[64,4,32,128]{3,2,0,1:T(8,128)(2,1)}), bf16[64,1,32,128]{3,2,0,1:T(8,128)(2,1)}) %reduce-scatter.3.cloned.1.call-update) | async-done | bytes 524304 | tf_op jit(solution)/shard_map/reduce_scatter | solution.py:117
  205.8 3.5 all-to-all-start.1
  209.3 0.3 all-reduce.3.cloned.1.call-start
  209.6 3.8 %fusion.49 = f32[128,128]{1,0:T(8,128)} fusion(bf16[8192,128]{1,0:T(8,128)(2,1)} %copy-done.4, bf16[8192,128]{1,0:T(8,128)(2,1)} %copy-done.9), kind=kOutput, calls=%fused_computation.110 | convolution fusion | flops 268435456 | bytes 4259840 | tf_op jit(solution)/shard_map/dot_general | solution.py:102
  213.4 1.4 fusion.50
  214.7 3.3 all-to-all-done.1
  218.1 0.1 convert_bitcast_fusion.4
  218.3 33.9 %reduce-scatter.5.cloned.1.call-done = bf16[2,16,128,128]{2,1,3,0:T(8,128)(2,1)} async-done(((bf16[2,64,128,128]{2,1,3,0:T(8,128)(2,1)}), bf16[2,16,128,128]{2,1,3,0:T(8,128)(2,1)}) %reduce-scatter.5.cloned.1.call-update) | async-done | bytes 1048592 | tf_op jit(solution)/shard_map/reduce_scatter | solution.py:132
  252.2 1.5 convert_reduce_fusion.3
  253.7 1.4 copy.76
  255.1 3.6 multiply_convert_fusion.6
  258.7 0.8 copy-done.13
  259.5 1.2 convolution_bitcast_fusion
  260.7 2.0 fusion.47
  262.8 0.3 fusion.24
  263.1 1.0 copy.78
  264.1 89.8 %all-reduce.3.cloned.1.call-done = (f32[128,512]{1,0:T(8,128)}, f32[128,128]{1,0:T(8,128)}, f32[128,128]{1,0:T(8,128)}) async-done(((f32[128,512]{1,0:T(8,128)}, f32[128,128]{1,0:T(8,128)}, f32[128,128]{1,0:T(8,128)}), (f32[128,512]{1,0:T(8,128)}, f32[128,128]{1,0:T(8,128)}, f32[128,128]{1,0:T(8,128)})) %all-reduce.3.cloned.1.call-update) | async-done | bytes 393232 | tf_op jit(solution)/shard_map/psum | solution.py:152
  353.9 1.7 copy.97
  355.6 1.5 copy.98
  357.0 1.5 copy.99
  (64 shorter events, 0.7 us)
Async XLA Ops:
  7.2 1.7 copy-start
  7.2 33.2 %all-gather.3.cloned.1.call-start = ((), (), s32[]{:S(2)}) async-start(), calls=%async_computation.4 | async-start | bytes 2621440 | tf_op jit(solution)/shard_map/all_gather | solution.py:81
  10.4 1.9 copy-start.1
  12.3 7.3 %copy-start.21 = (s32[1,2]{1,0:T(1,128)S(1)}, s32[1,2]{1,0:T(1,128)}, u32[]{:S(2)}) copy-start(s32[1,2]{1,0:T(1,128)} %param.15) | copy-start | bytes 28
  12.3 18.1 %copy-start.3 = (bf16[1,2,32,128,128]{4,3,2,1,0:T(8,128)(2,1)S(1)}, bf16[1,2,32,128,128]{4,3,2,1,0:T(8,128)(2,1)}, u32[]{:S(2)}) copy-start(bf16[1,2,32,128,128]{4,3,2,1,0:T(8,128)(2,1)} %param.13) | copy-start | bytes 6291460
  13.7 19.9 %copy-start.16 = (f32[128]{0:T(128)S(1)}, f32[128]{0:T(128)}, u32[]{:S(2)}) copy-start(f32[128]{0:T(128)} %param.17) | copy-start | bytes 1540
  13.7 19.9 %copy-start.17 = (f32[128]{0:T(128)S(1)}, f32[128]{0:T(128)}, u32[]{:S(2)}) copy-start(f32[128]{0:T(128)} %param.18) | copy-start | bytes 1540
  14.6 14.9 %all-to-all-start = ((bf16[4,16,1,32,128]{4,3,1,2,0:T(8,128)(2,1)}), bf16[4,16,1,32,128]{4,3,1,2,0:T(8,128)(2,1)S(1)}, u32[]{:S(2)}, u32[]{:S(2)}) async-start(bf16[4,16,1,32,128]{4,3,1,2,0:T(8,128)(2,1)} %pad_maximum_fusion.1), calls=%async_computation | async-start | bytes 1048576 | tf_op jit(solution)/shard_map/all_to_all | solution.py:65
  18.8 70.7 %all-gather.5.cloned.1.call-start = ((), (), s32[]{:S(2)}) async-start(), calls=%async_computation.5 | async-start | bytes 2621440 | tf_op jit(solution)/shard_map/all_gather | solution.py:79
  29.5 0.8 copy-start.11
  30.3 175.5 %reduce-scatter.3.cloned.1.call-start = ((), (), s32[]{:S(2)}) async-start(), calls=%async_computation.6 | async-start | bytes 2621440 | tf_op jit(solution)/shard_map/reduce_scatter | solution.py:117
  118.2 3.4 copy-start.2
  118.2 3.4 copy-start.15
  118.2 3.5 copy-start.18
  121.0 5.2 %copy-start.14 = (bf16[128,128]{1,0:T(8,128)(2,1)S(1)}, bf16[128,128]{1,0:T(8,128)(2,1)}, u32[]{:S(2)}) copy-start(bf16[128,128]{1,0:T(8,128)(2,1)} %param.22) | copy-start | bytes 98308
  126.2 1.3 copy-start.4
  126.2 2.3 copy-start.7
  126.2 3.0 copy-start.19
  126.2 3.0 copy-start.20
  133.5 6.2 %copy-start.9 = (bf16[8192,128]{1,0:T(8,128)(2,1)}, bf16[8192,128]{1,0:T(8,128)(2,1)S(1)}, u32[]{:S(2)}) copy-start(bf16[8192,128]{1,0:T(8,128)(2,1)S(1)} %get-tuple-element.43) | copy-start | bytes 6291460
  145.2 6.2 %copy-start.6 = (bf16[64,128,128,1]{1,0,3,2:T(8,128)(2,1)S(1)}, bf16[64,128,128,1]{1,0,3,2:T(8,128)(2,1)}, u32[]{:S(2)}) copy-start(bf16[64,128,128,1]{1,0,3,2:T(8,128)(2,1)} %copy.81) | copy-start | bytes 6291460
  150.0 1.4 copy-start.5
  163.1 89.1 %reduce-scatter.5.cloned.1.call-start = ((), (), s32[]{:S(2)}) async-start(), calls=%async_computation.7 | async-start | bytes 5242880 | tf_op jit(solution)/shard_map/reduce_scatter | solution.py:132
  189.5 23.8 %copy-start.8 = (bf16[8192,128]{1,0:T(8,128)(2,1)S(1)}, bf16[8192,128]{1,0:T(8,128)(2,1)}, u32[]{:S(2)}) copy-start(bf16[8192,128]{1,0:T(8,128)(2,1)} %add_convert_fusion.1) | copy-start | bytes 6291460
  205.8 12.3 %all-to-all-start.1 = ((bf16[4,16,32,128]{3,2,1,0:T(8,128)(2,1)}), bf16[4,16,32,128]{3,2,1,0:T(8,128)(2,1)S(1)}, u32[]{:S(2)}, u32[]{:S(2)}) async-start(bf16[4,16,32,128]{3,2,1,0:T(8,128)(2,1)} %bitcast.133), calls=%async_computation.2 | async-start | bytes 1048576 | tf_op jit(solution)/shard_map/all_to_all | solution.py:120
  209.3 144.6 %all-reduce.3.cloned.1.call-start = ((), (), s32[]{:S(2)}) async-start(), calls=%async_computation.8 | async-start | bytes 786432 | tf_op jit(solution)/shard_map/psum | solution.py:152
  209.6 3.8 %copy-start.10 = (bf16[8192,128]{1,0:T(8,128)(2,1)S(1)}, bf16[8192,128]{1,0:T(8,128)(2,1)}, u32[]{:S(2)}) copy-start(bf16[8192,128]{1,0:T(8,128)(2,1)} %get-tuple-element.41) | copy-start | bytes 6291460
  258.7 0.8 copy-start.13
  258.7 2.0 copy-start.12
Sparse Core Ops, SparseCore 0:
  13.8 26.5 all-gather.2
  42.6 46.9 all-gather.4
  163.2 42.5 reduce-scatter.2
  208.3 43.8 reduce-scatter.4
  262.9 90.9 all-reduce.2
